TPU v7x, 32 devices: a whole 2x2x4 slice. The times are simulated.
32 devices in a mesh: groups: 2 (over x), seq: 8 (over z, y), mp: 2 (over core).
Axes of the slice: x: 2, y: 2, z: 4, core: 2. Of those that a mesh axis runs over, the one named last changes fastest.
Arguments:
- queries: bfloat16 [8192, 4096], P(('groups', 'seq'), 'mp'), parts along dimension 0, may hold values from -6 to 6
- keys: bfloat16 [8192, 512], P(('groups', 'seq'), 'mp'), parts along dimension 0, may hold values from -6 to 6
- values: bfloat16 [8192, 512], P(('groups', 'seq'), 'mp'), parts along dimension 0, may hold values from -6 to 6
- feat_weight: bfloat16 [32, 128, 128], P('mp'), may hold values from -0.5 to 0.5
- head_gain: float32 [4096], P('mp'), may hold values from 0.1 to 1.9
- out_weight: bfloat16 [4096, 4096], P('mp'), may hold values from -0.09375 to 0.09375
Outputs:
- mixed: bfloat16 [8192, 4096], P(('groups', 'seq', 'mp')), parts along dimension 0
There are 2 independent parts, one for each index of `groups`. A program takes and returns all parts, laid end to end along the dimension named above; an argument that names none is the same for every part. Nothing has to cross between parts.
All inputs are finite; a program needn't handle non-finite values.
Results may differ from a plain program's by a relative error of at most 0.0083.
Values sent between devices are 32-bit elements; how exact they have to be, the bound alone decides.
A program may use at most 128 MiB of HBM per device.

v0:
```python
import jax
import jax.numpy as jnp
from jax import lax
from jax.sharding import PartitionSpec as P

HD = 128


def body(queries, keys, values, feat_weight, head_gain, out_weight):
    tok_rows = queries.shape[0]
    head_count = feat_weight.shape[0]
    pair_count = keys.shape[1] // HD
    group_size = head_count // pair_count
    query_heads = queries.reshape(tok_rows, head_count, HD)
    key_heads = keys.reshape(tok_rows, pair_count, HD)
    value_heads = values.reshape(tok_rows, pair_count, HD)
    grouped_weight = feat_weight.reshape(pair_count, group_size, HD, HD)
    mapped_query = jnp.einsum(
        "thd,hde->the", query_heads, feat_weight, preferred_element_type=jnp.float32
    )
    feat_query = (jax.nn.elu(mapped_query) + 1.0).astype(jnp.bfloat16)
    mapped_key = jnp.einsum(
        "tgd,gjde->tgje", key_heads, grouped_weight, preferred_element_type=jnp.float32
    )
    feat_key = (jax.nn.elu(mapped_key) + 1.0).astype(jnp.bfloat16)
    state_now = jnp.einsum(
        "tgjf,tgd->gjfd", feat_key, value_heads, preferred_element_type=jnp.float32
    )
    state_now = state_now.reshape(head_count, HD, HD)
    every_state = lax.all_gather(state_now[None], "seq", axis=0, tiled=True)
    earlier = jnp.arange(every_state.shape[0]) < lax.axis_index("seq")
    prefix = jnp.sum(jnp.where(earlier[:, None, None, None], every_state, 0.0), axis=0)
    feat_key_flat = feat_key.reshape(tok_rows, head_count, HD)
    scores = jnp.einsum(
        "thf,shf->hts", feat_query, feat_key_flat, preferred_element_type=jnp.float32
    )
    causal = jnp.arange(tok_rows)[:, None] >= jnp.arange(tok_rows)[None, :]
    scores = jnp.where(causal[None], scores, 0.0).astype(jnp.bfloat16)
    scores = scores.reshape(pair_count, group_size, tok_rows, tok_rows)
    intra_part = jnp.einsum(
        "gjts,sgd->tgjd", scores, value_heads, preferred_element_type=jnp.float32
    )
    intra_part = intra_part.reshape(tok_rows, head_count, HD)
    inter_part = jnp.einsum(
        "thf,hfd->thd", feat_query.astype(jnp.float32), prefix, precision=lax.Precision.HIGHEST
    )
    attn = inter_part + intra_part
    gain_heads = head_gain.reshape(head_count, HD)
    normed = attn * lax.rsqrt(jnp.mean(attn * attn, axis=-1, keepdims=True) + 1e-06) * gain_heads
    normed = normed.astype(jnp.bfloat16).reshape(tok_rows, head_count * HD)
    mixed = lax.psum_scatter(
        jnp.dot(normed, out_weight, preferred_element_type=jnp.float32),
        "mp",
        scatter_dimension=0,
        tiled=True,
    )
    return mixed.astype(jnp.bfloat16)


def solution(mesh):
    return jax.shard_map(
        body,
        mesh=mesh,
        in_specs=(
            P(("groups", "seq"), "mp"),
            P(("groups", "seq"), "mp"),
            P(("groups", "seq"), "mp"),
            P("mp", None, None),
            P("mp"),
            P("mp", None),
        ),
        out_specs=P(("groups", "seq", "mp"), None),
        check_vma=False,
    )
```

profile of v0, /device:TPU:27, one launch (start us, length us, event | category | flops | bytes accessed | tf_op | source)
XLA Modules:
  0.0 190.8 jit_solution(4243941409611703326)
XLA Ops:
  6.5 0.0 copy-start
  6.5 0.0 all-gather.2.cloned.1.call-start
  6.5 1.2 reshape.50
  7.7 1.0 reshape.51
  8.7 0.2 copy.34
  8.9 3.1 %fusion.2 = bf16[512,2,8,128]{0,3,2,1:T(8,128)(2,1)S(1)} fusion(bf16[2,8,128,128]{3,2,1,0:T(8,128)(2,1)} %bitcast.45, bf16[512,2,128,1]{2,1,0,3:T(2,128)(2,1)S(1)} %bitcast.43), kind=kOutput, calls=%fused_computation.8 | convolution fusion | flops 273678336 | bytes 2883584 | tf_op jit(solution)/shard_map/tgd,gjde->tgje/dot_general | solution.py:22
  12.0 0.0 copy-start.3
  12.0 1.3 copy-done.3
  13.3 1.7 fusion.9
  15.0 0.0 all-gather.2.cloned.1.call-update
  15.0 0.2 reduce-scatter.2.cloned.1.call-start
  15.3 0.1 iota_compare_fusion
  15.4 0.0 copy-done
  15.4 0.0 copy-done.8
  15.4 0.0 copy-start.4
  15.4 2.1 %fusion.5 = bf16[512,16,128]{0,2,1:T(8,128)(2,1)S(1)} fusion(bf16[16,128,128]{2,1,0:T(8,128)(2,1)S(1)} %copy-done.8, bf16[512,2048]{1,0:T(8,128)(2,1)S(1)} %copy-done), kind=kOutput, calls=%fused_computation.11 | convolution fusion | flops 273678336 | bytes 4718592 | tf_op jit(solution)/shard_map/thd,hde->the/dot_general | solution.py:18
  17.5 0.0 copy-start.5
  17.5 0.0 copy-done.4
  17.5 2.4 %select_convert_fusion = bf16[16,512,512]{2,1,0:T(8,128)(2,1)S(1)} fusion(bf16[512,16,128]{0,2,1:T(8,128)(2,1)S(1)} %fusion.5, bf16[512,16,128]{0,2,1:T(8,128)(2,1)S(1)} %bitcast.41, pred[512,512]{1,0:T(8,128)(4,1)S(1)} %iota_compare_fusion), kind=kOutput, calls=%fused_computation | convolution fusion | flops 1082130432 | bytes 12845056 | tf_op jit(solution)/shard_map/thf,shf->hts/dot_general | solution.py:34
  20.0 0.0 copy-done.5
  20.0 4.8 %fusion.10 = f32[2,8,512,128]{2,3,1,0:T(8,128)} fusion(bf16[2,8,512,512]{3,2,1,0:T(8,128)(2,1)S(1)} %bitcast.38, bf16[512,2,128,1]{0,2,3,1:T(8,128)(2,1)S(1)} %copy.34), kind=kOutput, calls=%fused_computation.22 | convolution fusion | flops 1073741824 | bytes 12845056 | tf_op jit(solution)/shard_map/gjts,sgd->tgjd/dot_general | solution.py:40
  24.7 114.6 %all-gather.2.cloned.1.call-done = f32[8,16,128,128]{3,2,1,0:T(8,128)} async-done(((f32[1,16,128,128]{3,2,1,0:T(8,128)}), f32[8,16,128,128]{3,2,1,0:T(8,128)}) %all-gather.2.cloned.1.call-update) | async-done | bytes 8388624 | tf_op jit(solution)/shard_map/all_gather | solution.py:30
  139.4 4.7 %select_reduce_fusion = f32[16,128,128]{2,1,0:T(8,128)S(1)} fusion(f32[8,16,128,128]{3,2,1,0:T(8,128)} %all-gather.2.cloned.1.call-done, pred[8]{0:T(512)(128)(4,1)S(1)} %iota_compare_fusion.1), kind=kLoop, calls=%fused_computation.5 | loop fusion | flops 3932160 | bytes 9437192 | tf_op jit(solution)/shard_map/reduce_sum | solution.py:32
  144.1 0.5 copy-done.6
  144.6 2.5 %multiply_reduce_fusion = (f32[512,16]{0,1:T(8,128)S(1)}, f32[512,16,128]{0,2,1:T(8,128)S(1)}) fusion(f32[2,8,512,128]{2,3,1,0:T(8,128)S(1)} %copy-done.2, f32[16,128,128]{2,1,0:T(8,128)S(1)} %select_reduce_fusion, bf16[512,16,128]{0,2,1:T(8,128)(2,1)S(1)} %copy-done.6), kind=kOutput, calls=%fused_computation.14 | convolution fusion | flops 1613750272 | bytes 11567104 | tf_op jit(solution)/shard_map/thf,hfd->thd/dot_general | solution.py:44
  147.2 0.0 copy-done.7
  147.2 0.6 multiply_convert_fusion
  147.8 14.8 %fusion.11 = f32[512,4096]{1,0:T(8,128)} fusion(bf16[512,2048]{0,1:T(8,128)(2,1)S(1)} %bitcast.40, bf16[2048,4096]{1,0:T(8,128)(2,1)} %param.11), kind=kOutput, calls=%fused_computation.23 | convolution fusion | flops 8589934592 | bytes 27262976 | tf_op jit(solution)/shard_map/dot_general | solution.py:52
  162.6 0.0 reduce-scatter.2.cloned.1.call-update
  162.6 0.0 copy-start.1
  162.6 17.6 %reduce-scatter.2.cloned.1.call-done = f32[256,4096]{1,0:T(8,128)} async-done(((f32[512,4096]{1,0:T(8,128)}), f32[256,4096]{1,0:T(8,128)}) %reduce-scatter.2.cloned.1.call-update) | async-done | bytes 4194320 | tf_op jit(solution)/shard_map/reduce_scatter | solution.py:51
  180.2 3.8 %convert_element_type.20 = bf16[256,4096]{1,0:T(8,128)(2,1)} convert(f32[256,4096]{1,0:T(8,128)} %reduce-scatter.2.cloned.1.call-done) | non-fusion elementwise | flops 1048576 | bytes 6291456 | tf_op jit(solution)/shard_map/convert_element_type | solution.py:57
  (8 shorter events, 0.0 us)
Async XLA Ops:
  6.5 8.8 %copy-start = (bf16[512,2048]{1,0:T(8,128)(2,1)S(1)}, bf16[512,2048]{1,0:T(8,128)(2,1)}, u32[]{:S(2)}) copy-start(bf16[512,2048]{1,0:T(8,128)(2,1)} %param.6) | copy-start | bytes 6291460
  6.5 132.8 %all-gather.2.cloned.1.call-start = ((), (), s32[]{:S(2)}) async-start(), calls=%async_computation.1 | async-start | bytes 9437184 | tf_op jit(solution)/shard_map/all_gather | solution.py:30
  12.0 1.3 copy-start.3
  13.3 2.1 %copy-start.8 = (bf16[16,128,128]{2,1,0:T(8,128)(2,1)S(1)}, bf16[16,128,128]{2,1,0:T(8,128)(2,1)}, u32[]{:S(2)}) copy-start(bf16[16,128,128]{2,1,0:T(8,128)(2,1)} %param.9) | copy-start | bytes 1572868
  15.0 165.1 %reduce-scatter.2.cloned.1.call-start = ((), (), s32[]{:S(2)}) async-start(), calls=%async_computation.2 | async-start | bytes 12582912 | tf_op jit(solution)/shard_map/reduce_scatter | solution.py:51
  15.4 2.1 %copy-start.4 = (bf16[512,2,8,128]{0,3,2,1:T(8,128)(2,1)S(1)}, bf16[512,2,8,128]{0,3,2,1:T(8,128)(2,1)}, u32[]{:S(2)}) copy-start(bf16[512,2,8,128]{0,3,2,1:T(8,128)(2,1)} %copy-done.3) | copy-start | bytes 6291460
  17.5 2.5 %copy-start.5 = (bf16[512,16,128]{0,2,1:T(8,128)(2,1)}, bf16[512,16,128]{0,2,1:T(8,128)(2,1)S(1)}, u32[]{:S(2)}) copy-start(bf16[512,16,128]{0,2,1:T(8,128)(2,1)S(1)} %fusion.5) | copy-start | bytes 6291460
  139.4 4.7 %copy-start.2 = (f32[2,8,512,128]{2,3,1,0:T(8,128)S(1)}, f32[2,8,512,128]{2,3,1,0:T(8,128)}, u32[]{:S(2)}) copy-start(f32[2,8,512,128]{2,3,1,0:T(8,128)} %fusion.10) | copy-start | bytes 12582916
  139.4 5.3 %copy-start.6 = (bf16[512,16,128]{0,2,1:T(8,128)(2,1)S(1)}, bf16[512,16,128]{0,2,1:T(8,128)(2,1)}, u32[]{:S(2)}) copy-start(bf16[512,16,128]{0,2,1:T(8,128)(2,1)} %copy-done.5) | copy-start | bytes 6291460
  144.6 2.5 %copy-start.7 = (f32[2048]{0:T(1024)S(1)}, f32[2048]{0:T(1024)}, u32[]{:S(2)}) copy-start(f32[2048]{0:T(1024)} %param.10) | copy-start | bytes 24580
  162.6 21.4 %copy-start.1 = (bf16[512,2048]{1,0:T(8,128)(2,1)S(1)}, bf16[512,2048]{1,0:T(8,128)(2,1)}, u32[]{:S(2)}) copy-start(bf16[512,2048]{1,0:T(8,128)(2,1)} %param.6) | copy-start | bytes 6291460
Sparse Core Ops, SparseCore 0:
  15.2 124.1 all-gather.1
  162.7 17.4 reduce-scatter.1
where the time goes:
time: 192 us; the launch traced here: 191 us
  waiting for transfers between devices  132 us (69%)
  matrix products  31.4 us (16%)
  between operations  13.6 us (7%)
  other arithmetic  9.22 us (5%)
  local copies, waits for them, and re-layouts  4.19 us (2%)
    all_gather x1, waiting for transfers between devices, body(): every_state = lax.all_gather(state_now[None], 'seq', axis=0, tiled=True)  115 us
    reduce_scatter x1, waiting for transfers between devices, body(): lax.psum_scatter(jnp.dot(normed, out_weight, preferred_element_type=jnp.f...  17.6 us
    dot_general x1, matrix products, body(): jnp.dot(normed, out_weight, preferred_element_type=jnp.float32)  14.8 us
    dot_general x1, matrix products, body(): jnp.einsum('gjts,sgd->tgjd', scores, value_heads, preferred_element_type=...  4.77 us
    reduce_sum x1, other arithmetic, body(): jnp.sum(jnp.where(earlier[:, None, None, None], every_state, 0.0), axis=0)  4.74 us
  transfers between devices with their start and end apart: 2, of which 2 were waited for; matrix products, arithmetic and copies ran while one was open for 5% of the time, Pallas kernels for 0%

commit v1 on v0

v1 whole, which is shorter than its diff:
```python
import functools

import jax
import jax.numpy as jnp
from jax import lax
from jax.experimental import pallas as pl
from jax.experimental.pallas import tpu as pltpu
from jax.sharding import PartitionSpec as P

HD = 128
PAIR = 2 * HD
COLS = 512
MESH = pl.DeviceIdType.MESH
NT = (((1,), (1,)), ((), ()))


def feature(mapped):
    return jnp.where(mapped > 0.0, mapped + 1.0, jnp.exp(jnp.minimum(mapped, 0.0))).astype(jnp.bfloat16)


def kernel(
    n_seq, q_hbm, k_hbm, v_hbm, fw_hbm, gain_hbm, w_hbm, out_hbm,
    q_buf, k_buf, v_buf, fw_buf, gain_buf, w_buf, out_buf,
    fk_buf, fq_buf, intra_buf, nrm_buf, acc,
    s_buf, peer_s, p_buf, fwd, mp_recv,
    q_sem, kv_sem, w_sem, out_sem,
    y_send, y_recv, z_send, z_recv, mp_send, mp_recv_sem,
):
    grp = lax.axis_index("groups")
    me = lax.axis_index("seq")
    mp = lax.axis_index("mp")
    layer = lax.div(me, 2)
    side = lax.rem(me, 2)
    mate = (grp, me + 1 - 2 * side, mp)
    up = (grp, me + 2, mp)
    down = (grp, me - 2, mp)
    other_mp = 1 - mp
    peer = (grp, me, other_mp)
    has_down = layer > 0
    has_up = me + 2 < n_seq
    n_pairs = q_buf.shape[0]
    rows = q_buf.shape[1]
    half = rows // 2
    n_cols = acc.shape[0]
    n_kv = k_buf.shape[1] // HD
    pairs_kv = n_pairs // n_kv

    def k_copy():
        return pltpu.make_async_copy(k_hbm, k_buf, kv_sem.at[0])

    def v_copy():
        return pltpu.make_async_copy(v_hbm, v_buf, kv_sem.at[1])

    def fw_copy():
        return pltpu.make_async_copy(fw_hbm, fw_buf, kv_sem.at[2])

    def gain_copy():
        return pltpu.make_async_copy(gain_hbm, gain_buf, kv_sem.at[3])

    def q_copy(i):
        at = pl.multiple_of(i * PAIR, PAIR)
        return pltpu.make_async_copy(q_hbm.at[:, pl.ds(at, PAIR)], q_buf.at[i], q_sem.at[i])

    def w_copy(i):
        at = pl.multiple_of(i * PAIR, PAIR)
        return pltpu.make_async_copy(w_hbm.at[pl.ds(at, PAIR), :], w_buf.at[i], w_sem.at[i])

    def y_copy(i):
        return pltpu.make_async_remote_copy(
            src_ref=s_buf.at[i], dst_ref=peer_s.at[i], send_sem=y_send.at[i],
            recv_sem=y_recv.at[i], device_id=mate, device_id_type=MESH)

    def z_copy(i):
        return pltpu.make_async_remote_copy(
            src_ref=fwd.at[i], dst_ref=p_buf.at[i], send_sem=z_send.at[i],
            recv_sem=z_recv.at[i], device_id=up, device_id_type=MESH)

    def mp_copy(c):
        return pltpu.make_async_remote_copy(
            src_ref=acc.at[c, pl.ds(pl.multiple_of(other_mp * half, half), half)],
            dst_ref=mp_recv.at[c], send_sem=mp_send.at[c],
            recv_sem=mp_recv_sem.at[c], device_id=peer, device_id_type=MESH)

    def out_copy(c):
        at = pl.multiple_of(c * COLS, COLS)
        return pltpu.make_async_copy(out_buf.at[c], out_hbm.at[:, pl.ds(at, COLS)], out_sem.at[c])

    k_copy().start()
    fw_copy().start()
    v_copy().start()
    gain_copy().start()

    @pl.loop(0, n_pairs)
    def _(i):
        q_copy(i).start()

    @pl.loop(0, n_pairs)
    def _(i):
        w_copy(i).start()

    barrier = pltpu.get_barrier_semaphore()
    pl.semaphore_signal(barrier, inc=1, device_id=mate, device_id_type=MESH)
    pl.semaphore_signal(barrier, inc=1, device_id=peer, device_id_type=MESH)

    @pl.when(has_up)
    def _():
        pl.semaphore_signal(barrier, inc=1, device_id=up, device_id_type=MESH)

    @pl.when(has_down)
    def _():
        pl.semaphore_signal(barrier, inc=1, device_id=down, device_id_type=MESH)

    pl.semaphore_wait(barrier, 2 + has_up.astype(jnp.int32) + has_down.astype(jnp.int32))

    @pl.when(jnp.logical_not(has_down))
    def _():
        p_buf[...] = jnp.zeros_like(p_buf)

    k_copy().wait()
    fw_copy().wait()
    v_copy().wait()

    for g in range(n_kv):
        keys = k_buf[:, g * HD:(g + 1) * HD]
        values_t = v_buf[:, g * HD:(g + 1) * HD].T

        @pl.loop(g * pairs_kv, (g + 1) * pairs_kv)
        def _(i):
            weight = jnp.concatenate([fw_buf[2 * i], fw_buf[2 * i + 1]], axis=1)
            fk = feature(jnp.dot(keys, weight, preferred_element_type=jnp.float32))
            fk_buf[i] = fk
            s_buf[i] = jnp.dot(values_t, fk, preferred_element_type=jnp.float32)
            y_copy(i).start()

    gain_copy().wait()

    def intra(i):
        q_copy(i).wait()
        zero = jnp.zeros((HD, HD), jnp.bfloat16)
        weight = jnp.concatenate(
            [jnp.concatenate([fw_buf[2 * i], zero], axis=1),
             jnp.concatenate([zero, fw_buf[2 * i + 1]], axis=1)], axis=0)
        fq = feature(jnp.dot(q_buf[i], weight, preferred_element_type=jnp.float32))
        fq_buf[i] = fq
        kv_at = pl.multiple_of(lax.div(i, pairs_kv) * HD, HD)
        values = v_buf[:, pl.ds(kv_at, HD)]
        causal = (lax.broadcasted_iota(jnp.int32, (half, half), 0)
                  >= lax.broadcasted_iota(jnp.int32, (half, half), 1))
        for j in range(2):
            lanes = slice(j * HD, (j + 1) * HD)
            fk_h = fk_buf[i, :, lanes]
            fq_h = fq[:, lanes]
            top = lax.dot_general(fq_h[:half], fk_h[:half], NT, preferred_element_type=jnp.float32)
            top = jnp.where(causal, top, 0.0).astype(jnp.bfloat16)
            intra_buf[i, :half, lanes] = jnp.dot(top, values[:half], preferred_element_type=jnp.float32)
            left = lax.dot_general(fq_h[half:], fk_h[:half], NT, preferred_element_type=jnp.float32)
            right = lax.dot_general(fq_h[half:], fk_h[half:], NT, preferred_element_type=jnp.float32)
            right = jnp.where(causal, right, 0.0)
            low = jnp.concatenate([left.astype(jnp.bfloat16), right.astype(jnp.bfloat16)], axis=1)
            intra_buf[i, half:, lanes] = jnp.dot(low, values, preferred_element_type=jnp.float32)

    def serve(i):
        y_copy(i).wait_recv()

        @pl.when(has_down)
        def _():
            z_copy(i).wait_recv()

        @pl.when(has_up)
        def _():
            fwd[i] = p_buf[i] + s_buf[i] + peer_s[i]
            z_copy(i).start()

    def finish(i):
        prefix = p_buf[i] + jnp.where(side == 1, peer_s[i], 0.0)
        high = prefix.astype(jnp.bfloat16)
        low = (prefix - high.astype(jnp.float32)).astype(jnp.bfloat16)
        for j in range(2):
            lanes = slice(j * HD, (j + 1) * HD)
            fq_h = fq_buf[i, :, lanes]
            inter = lax.dot_general(
                jnp.concatenate([fq_h, fq_h], axis=1),
                jnp.concatenate([high[:, lanes], low[:, lanes]], axis=1),
                NT, preferred_element_type=jnp.float32)
            attn = inter + intra_buf[i, :, lanes]
            scale = lax.rsqrt(jnp.mean(attn * attn, axis=-1, keepdims=True) + 1e-06)
            gain = gain_buf[pl.ds(2 * i + j, 1), :]
            nrm_buf[:, lanes] = (attn * scale * gain).astype(jnp.bfloat16)

    def project(i):
        w_copy(i).wait()

        @pl.when(i == 0)
        def _():
            @pl.loop(0, n_cols)
            def _(c):
                at = pl.multiple_of(c * COLS, COLS)
                acc[c] = jnp.dot(nrm_buf[...], w_buf[i, :, pl.ds(at, COLS)], preferred_element_type=jnp.float32)

        @pl.when(i > 0)
        def _():
            @pl.loop(0, n_cols)
            def _(c):
                at = pl.multiple_of(c * COLS, COLS)
                acc[c] += jnp.dot(nrm_buf[...], w_buf[i, :, pl.ds(at, COLS)], preferred_element_type=jnp.float32)

    last = n_pairs - 1

    @pl.loop(0, n_pairs + n_seq // 2 - 1)
    def _(t):
        @pl.when(t < n_pairs)
        def _():
            intra(t)

        i = t - layer

        @pl.when(jnp.logical_and(i >= 0, i < n_pairs))
        def _():
            serve(i)
            finish(i)

            @pl.when(i < last)
            def _():
                project(i)

    w_copy(last).wait()
    theirs = pl.ds(pl.multiple_of(other_mp * half, half), half)
    mine = pl.ds(pl.multiple_of(mp * half, half), half)

    @pl.loop(0, n_cols)
    def _(c):
        at = pl.multiple_of(c * COLS, COLS)
        acc[c, theirs] += jnp.dot(nrm_buf[theirs], w_buf[last, :, pl.ds(at, COLS)], preferred_element_type=jnp.float32)
        mp_copy(c).start()

    @pl.loop(0, n_cols)
    def _(c):
        at = pl.multiple_of(c * COLS, COLS)
        total = acc[c, mine] + jnp.dot(nrm_buf[mine], w_buf[last, :, pl.ds(at, COLS)], preferred_element_type=jnp.float32)
        mp_copy(c).wait_recv()
        out_buf[c] = (total + mp_recv[c]).astype(jnp.bfloat16)
        out_copy(c).start()

    @pl.loop(0, n_pairs)
    def _(i):
        y_copy(i).wait_send()

        @pl.when(has_up)
        def _():
            z_copy(i).wait_send()

    @pl.loop(0, n_cols)
    def _(c):
        mp_copy(c).wait_send()
        out_copy(c).wait()


def body(n_seq, queries, keys, values, feat_weight, head_gain, out_weight):
    rows, feats = queries.shape
    heads = feat_weight.shape[0]
    n_pairs = heads // 2
    dout = out_weight.shape[1]
    n_cols = dout // COLS
    half = rows // 2
    bf, f32 = jnp.bfloat16, jnp.float32
    gain = head_gain.reshape(heads, HD)
    dma = pltpu.SemaphoreType.DMA
    return pl.pallas_call(
        functools.partial(kernel, n_seq),
        out_shape=jax.ShapeDtypeStruct((half, dout), bf),
        in_specs=[pl.BlockSpec(memory_space=pl.ANY)] * 6,
        out_specs=pl.BlockSpec(memory_space=pl.ANY),
        scratch_shapes=[
            pltpu.VMEM((n_pairs, rows, PAIR), bf),
            pltpu.VMEM(keys.shape, bf),
            pltpu.VMEM(values.shape, bf),
            pltpu.VMEM(feat_weight.shape, bf),
            pltpu.VMEM((heads, HD), f32),
            pltpu.VMEM((n_pairs, PAIR, dout), bf),
            pltpu.VMEM((n_cols, half, COLS), bf),
            pltpu.VMEM((n_pairs, rows, PAIR), bf),
            pltpu.VMEM((n_pairs, rows, PAIR), bf),
            pltpu.VMEM((n_pairs, rows, PAIR), f32),
            pltpu.VMEM((rows, PAIR), bf),
            pltpu.VMEM((n_cols, rows, COLS), f32),
            pltpu.VMEM((n_pairs, HD, PAIR), f32),
            pltpu.VMEM((n_pairs, HD, PAIR), f32),
            pltpu.VMEM((n_pairs, HD, PAIR), f32),
            pltpu.VMEM((n_pairs, HD, PAIR), f32),
            pltpu.VMEM((n_cols, half, COLS), f32),
            dma((n_pairs,)), dma((4,)), dma((n_pairs,)), dma((n_cols,)),
            dma((n_pairs,)), dma((n_pairs,)), dma((n_pairs,)), dma((n_pairs,)),
            dma((n_cols,)), dma((n_cols,)),
        ],
        compiler_params=pltpu.CompilerParams(
            collective_id=0, has_side_effects=True, vmem_limit_bytes=60 * 1024 * 1024),
        cost_estimate=pl.CostEstimate(
            flops=2 * rows * feats * dout, bytes_accessed=feats * dout * 2, transcendentals=0),
    )(queries, keys, values, feat_weight, gain, out_weight)


def solution(mesh):
    return jax.shard_map(
        functools.partial(body, mesh.shape["seq"]),
        mesh=mesh,
        in_specs=(
            P(("groups", "seq"), "mp"),
            P(("groups", "seq"), "mp"),
            P(("groups", "seq"), "mp"),
            P("mp", None, None),
            P("mp"),
            P("mp", None),
        ),
        out_specs=P(("groups", "seq", "mp"), None),
        check_vma=False,
    )
```

time: 192 us -> 59.3 us (0.31)
  waiting for transfers between devices: 132 us -> 0 us
  Pallas kernels: 0 us -> 56.1 us
  matrix products: 31.4 us -> 0 us
  between operations: 13.6 us -> 0.01 us
  other arithmetic: 9.22 us -> 0 us
    all_gather x1 -> x0, waiting for transfers between devices: 115 us -> none  [body(): every_state = lax.all_gather(state_now[None], 'seq', axis=0, tiled=True)]
    pallas_call x0 -> x1, Pallas kernels: none -> 56.1 us  [body(): pl.pallas_call(functools.partial(kernel, n_seq), out_shape=jax.ShapeDtype...]
    dot_general x7 -> x0, matrix products: 31.4 us -> none  [the longest x1 14.8 us: body(): jnp.dot(normed, out_weight, preferred_element_type=jnp.float32)]
    reduce_scatter x1 -> x0, waiting for transfers between devices: 17.6 us -> none  [body(): lax.psum_scatter(jnp.dot(normed, out_weight, preferred_element_type=jnp.f...]
    reduce_sum x1 -> x0, other arithmetic: 4.74 us -> none  [body(): jnp.sum(jnp.where(earlier[:, None, None, None], every_state, 0.0), axis=0)]
    convert_element_type x2 -> x0, other arithmetic: 4.38 us -> none  [the longest x1 3.79 us: body(): return mixed.astype(jnp.bfloat16)]
    reshape x3 -> x0, local copies, waits for them, and re-layouts: 2.34 us -> none  [the longest x2 1.18 us: body(): value_heads = values.reshape(tok_rows, pair_count, HD)]
  transfers between devices with their start and end apart: 2 -> 0, of which waited for: 2 -> 0; matrix products, arithmetic and copies ran while one was open for 5% -> 0% of each run, Pallas kernels for 0% -> 0%
where the time goes in v1:
time: 59.3 us; the launch traced here: 59.2 us
  Pallas kernels  56.1 us (95%)
  local copies, waits for them, and re-layouts  3.13 us (5%)
    pallas_call x1, Pallas kernels, body(): pl.pallas_call(functools.partial(kernel, n_seq), out_shape=jax.ShapeDtype...  56.1 us
    unnamed x1, local copies, waits for them, and re-layouts  3.13 us

profile of v1, /device:TPU:27, one launch (start us, length us, event | category | flops | bytes accessed | tf_op | source)
XLA Modules:
  0.0 59.2 jit_solution(13503029195922193299)
XLA Ops:
  0.0 56.1 %shard_map.64 = bf16[256,4096]{1,0:T(8,128)(2,1)} custom-call(bf16[512,2048]{1,0:T(8,128)(2,1)} %q_hbm.1, bf16[512,256]{1,0:T(8,128)(2,1)} %k_hbm.1, bf16[512,256]{1,0:T(8,128)(2,1)} %v_hbm.1, bf16[16,128,128]{2,1,0:T(8,128)(2,1)} %fw_hbm.1, f32[16,128]{1,0:T(8,128)} %bitcast.1, bf16[2048,4096]{1,0:T(8,128)(2,1)} %w_hbm.1), custom_call_target="tpu_custom_call" | custom-call | flops 8589934592 | bytes 16777216 | tf_op jit(solution)/shard_map/pallas_call | solution.py:268
  56.1 3.1 %copy.8 = bf16[256,4096]{1,0:T(8,128)(2,1)} copy(bf16[256,4096]{1,0:T(8,128)(2,1)} %shard_map.64) | data formatting | bytes 4194304

commit v2 on v1

--- a/solution.py
+++ b/solution.py
@@ -21,10 +21,10 @@
 def kernel(
     n_seq, q_hbm, k_hbm, v_hbm, fw_hbm, gain_hbm, w_hbm, out_hbm,
     q_buf, k_buf, v_buf, fw_buf, gain_buf, w_buf, out_buf,
-    fk_buf, fq_buf, intra_buf, nrm_buf, acc,
-    s_buf, peer_s, p_buf, fwd, mp_recv,
+    vt_buf, fk_buf, fq_buf, intra_buf, nrm_buf, acc,
+    s_buf, peer_s, p_buf, fwd, pre_out, pre_in, mp_recv,
     q_sem, kv_sem, w_sem, out_sem,
-    y_send, y_recv, z_send, z_recv, mp_send, mp_recv_sem,
+    y_send, y_recv, z_send, z_recv, b_send, b_recv, mp_send, mp_recv_sem,
 ):
     grp = lax.axis_index("groups")
     me = lax.axis_index("seq")
@@ -44,6 +44,10 @@
     n_cols = acc.shape[0]
     n_kv = k_buf.shape[1] // HD
     pairs_kv = n_pairs // n_kv
+    own_pairs = n_pairs // 2
+    own_heads = 2 * own_pairs
+    own_at = side * own_pairs
+    mate_at = own_pairs - own_at
 
     def k_copy():
         return pltpu.make_async_copy(k_hbm, k_buf, kv_sem.at[0])
@@ -63,17 +67,22 @@
 
     def w_copy(i):
         at = pl.multiple_of(i * PAIR, PAIR)
-        return pltpu.make_async_copy(w_hbm.at[pl.ds(at, PAIR), :], w_buf.at[i], w_sem.at[i])
+        return pltpu.make_async_copy(w_hbm.at[pl.ds(at, PAIR), :], w_buf.at[lax.div(i, own_pairs), pl.ds(pl.multiple_of(lax.rem(i, own_pairs) * PAIR, PAIR), PAIR)], w_sem.at[i])
 
     def y_copy(i):
         return pltpu.make_async_remote_copy(
-            src_ref=s_buf.at[i], dst_ref=peer_s.at[i], send_sem=y_send.at[i],
+            src_ref=s_buf.at[2 * mate_at + i], dst_ref=peer_s.at[i], send_sem=y_send.at[i],
             recv_sem=y_recv.at[i], device_id=mate, device_id_type=MESH)
 
     def z_copy(i):
         return pltpu.make_async_remote_copy(
             src_ref=fwd.at[i], dst_ref=p_buf.at[i], send_sem=z_send.at[i],
             recv_sem=z_recv.at[i], device_id=up, device_id_type=MESH)
+
+    def b_copy(i):
+        return pltpu.make_async_remote_copy(
+            src_ref=pre_out.at[i], dst_ref=pre_in.at[i], send_sem=b_send.at[i],
+            recv_sem=b_recv.at[i], device_id=mate, device_id_type=MESH)
 
     def mp_copy(c):
         return pltpu.make_async_remote_copy(
@@ -120,17 +129,27 @@
     fw_copy().wait()
     v_copy().wait()
 
+    def states(i):
+        kv_at = pl.multiple_of(lax.div(i, pairs_kv) * HD, HD)
+        weight = jnp.concatenate([fw_buf[2 * i], fw_buf[2 * i + 1]], axis=1)
+        fk = feature(jnp.dot(k_buf[:, pl.ds(kv_at, HD)], weight, preferred_element_type=jnp.float32))
+        fk_buf[i] = fk
+        state = jnp.dot(vt_buf[lax.div(i, pairs_kv)], fk, preferred_element_type=jnp.float32)
+        s_buf[2 * i] = state[:, :HD]
+        s_buf[2 * i + 1] = state[:, HD:]
+
     for g in range(n_kv):
-        keys = k_buf[:, g * HD:(g + 1) * HD]
-        values_t = v_buf[:, g * HD:(g + 1) * HD].T
-
-        @pl.loop(g * pairs_kv, (g + 1) * pairs_kv)
-        def _(i):
-            weight = jnp.concatenate([fw_buf[2 * i], fw_buf[2 * i + 1]], axis=1)
-            fk = feature(jnp.dot(keys, weight, preferred_element_type=jnp.float32))
-            fk_buf[i] = fk
-            s_buf[i] = jnp.dot(values_t, fk, preferred_element_type=jnp.float32)
-            y_copy(i).start()
+        vt_buf[g] = v_buf[:, g * HD:(g + 1) * HD].T
+
+    @pl.loop(0, own_pairs)
+    def _(t):
+        states(mate_at + t)
+        y_copy(2 * t).start()
+        y_copy(2 * t + 1).start()
+
+    @pl.loop(0, own_pairs)
+    def _(t):
+        states(own_at + t)
 
     gain_copy().wait()
 
@@ -159,91 +178,99 @@
             low = jnp.concatenate([left.astype(jnp.bfloat16), right.astype(jnp.bfloat16)], axis=1)
             intra_buf[i, half:, lanes] = jnp.dot(low, values, preferred_element_type=jnp.float32)
 
-    def serve(i):
-        y_copy(i).wait_recv()
+    def serve(k):
+        y_copy(k).wait_recv()
 
         @pl.when(has_down)
         def _():
-            z_copy(i).wait_recv()
+            z_copy(k).wait_recv()
 
         @pl.when(has_up)
         def _():
-            fwd[i] = p_buf[i] + s_buf[i] + peer_s[i]
-            z_copy(i).start()
-
-    def finish(i):
-        prefix = p_buf[i] + jnp.where(side == 1, peer_s[i], 0.0)
-        high = prefix.astype(jnp.bfloat16)
-        low = (prefix - high.astype(jnp.float32)).astype(jnp.bfloat16)
+            fwd[k] = p_buf[k] + s_buf[2 * own_at + k] + peer_s[k]
+            z_copy(k).start()
+
+        pre_out[k] = p_buf[k] + jnp.where(side == 0, s_buf[2 * own_at + k], 0.0)
+        b_copy(k).start()
+
+    def finish(i, grp_at, prefixes):
         for j in range(2):
             lanes = slice(j * HD, (j + 1) * HD)
+            high = prefixes[j].astype(jnp.bfloat16)
+            low = (prefixes[j] - high.astype(jnp.float32)).astype(jnp.bfloat16)
             fq_h = fq_buf[i, :, lanes]
             inter = lax.dot_general(
                 jnp.concatenate([fq_h, fq_h], axis=1),
-                jnp.concatenate([high[:, lanes], low[:, lanes]], axis=1),
+                jnp.concatenate([high, low], axis=1),
                 NT, preferred_element_type=jnp.float32)
             attn = inter + intra_buf[i, :, lanes]
             scale = lax.rsqrt(jnp.mean(attn * attn, axis=-1, keepdims=True) + 1e-06)
             gain = gain_buf[pl.ds(2 * i + j, 1), :]
-            nrm_buf[:, lanes] = (attn * scale * gain).astype(jnp.bfloat16)
-
-    def project(i):
-        w_copy(i).wait()
-
-        @pl.when(i == 0)
-        def _():
-            @pl.loop(0, n_cols)
-            def _(c):
-                at = pl.multiple_of(c * COLS, COLS)
-                acc[c] = jnp.dot(nrm_buf[...], w_buf[i, :, pl.ds(at, COLS)], preferred_element_type=jnp.float32)
-
-        @pl.when(i > 0)
-        def _():
-            @pl.loop(0, n_cols)
-            def _(c):
-                at = pl.multiple_of(c * COLS, COLS)
-                acc[c] += jnp.dot(nrm_buf[...], w_buf[i, :, pl.ds(at, COLS)], preferred_element_type=jnp.float32)
-
-    last = n_pairs - 1
-
-    @pl.loop(0, n_pairs + n_seq // 2 - 1)
+            at = pl.multiple_of(lax.rem(i, own_pairs) * PAIR + j * HD, HD)
+            nrm_buf[grp_at, :, pl.ds(at, HD)] = (attn * scale * gain).astype(jnp.bfloat16)
+
+    def finish_own(m):
+        finish(own_at + m, side, [
+            p_buf[2 * m + j] + jnp.where(side == 1, peer_s[2 * m + j], 0.0) for j in range(2)])
+
+    def finish_mate(m):
+        b_copy(2 * m).wait_recv()
+        b_copy(2 * m + 1).wait_recv()
+        finish(mate_at + m, 1 - side, [pre_in[2 * m], pre_in[2 * m + 1]])
+
+    @pl.loop(0, own_heads + n_seq // 2 - 1)
     def _(t):
         @pl.when(t < n_pairs)
         def _():
-            intra(t)
-
-        i = t - layer
-
-        @pl.when(jnp.logical_and(i >= 0, i < n_pairs))
-        def _():
-            serve(i)
-            finish(i)
-
-            @pl.when(i < last)
+            intra(lax.rem(own_at + t, n_pairs))
+
+        k = t - layer
+
+        @pl.when(jnp.logical_and(k >= 0, k < own_heads))
+        def _():
+            serve(k)
+
+            @pl.when(lax.rem(k, 2) == 1)
             def _():
-                project(i)
-
-    w_copy(last).wait()
+                finish_own(lax.div(k, 2))
+
+    @pl.loop(0, n_pairs)
+    def _(i):
+        w_copy(i).wait()
+
+    cols_each = n_cols // own_pairs
+
+    @pl.loop(0, own_pairs)
+    def _(m):
+        @pl.loop(m * cols_each, (m + 1) * cols_each)
+        def _(c):
+            at = pl.multiple_of(c * COLS, COLS)
+            acc[c] = jnp.dot(nrm_buf[side], w_buf[side, :, pl.ds(at, COLS)], preferred_element_type=jnp.float32)
+
+        finish_mate(m)
+
     theirs = pl.ds(pl.multiple_of(other_mp * half, half), half)
     mine = pl.ds(pl.multiple_of(mp * half, half), half)
+    rest = 1 - side
 
     @pl.loop(0, n_cols)
     def _(c):
         at = pl.multiple_of(c * COLS, COLS)
-        acc[c, theirs] += jnp.dot(nrm_buf[theirs], w_buf[last, :, pl.ds(at, COLS)], preferred_element_type=jnp.float32)
+        acc[c, theirs] += jnp.dot(nrm_buf[rest, theirs], w_buf[rest, :, pl.ds(at, COLS)], preferred_element_type=jnp.float32)
         mp_copy(c).start()
 
     @pl.loop(0, n_cols)
     def _(c):
         at = pl.multiple_of(c * COLS, COLS)
-        total = acc[c, mine] + jnp.dot(nrm_buf[mine], w_buf[last, :, pl.ds(at, COLS)], preferred_element_type=jnp.float32)
+        total = acc[c, mine] + jnp.dot(nrm_buf[rest, mine], w_buf[rest, :, pl.ds(at, COLS)], preferred_element_type=jnp.float32)
         mp_copy(c).wait_recv()
         out_buf[c] = (total + mp_recv[c]).astype(jnp.bfloat16)
         out_copy(c).start()
 
-    @pl.loop(0, n_pairs)
+    @pl.loop(0, own_heads)
     def _(i):
         y_copy(i).wait_send()
+        b_copy(i).wait_send()
 
         @pl.when(has_up)
         def _():
@@ -276,20 +303,24 @@
             pltpu.VMEM(values.shape, bf),
             pltpu.VMEM(feat_weight.shape, bf),
             pltpu.VMEM((heads, HD), f32),
-            pltpu.VMEM((n_pairs, PAIR, dout), bf),
+            pltpu.VMEM((2, feats // 2, dout), bf),
             pltpu.VMEM((n_cols, half, COLS), bf),
+            pltpu.VMEM((keys.shape[1] // HD, HD, rows), bf),
             pltpu.VMEM((n_pairs, rows, PAIR), bf),
             pltpu.VMEM((n_pairs, rows, PAIR), bf),
             pltpu.VMEM((n_pairs, rows, PAIR), f32),
-            pltpu.VMEM((rows, PAIR), bf),
+            pltpu.VMEM((2, rows, feats // 2), bf),
             pltpu.VMEM((n_cols, rows, COLS), f32),
-            pltpu.VMEM((n_pairs, HD, PAIR), f32),
-            pltpu.VMEM((n_pairs, HD, PAIR), f32),
-            pltpu.VMEM((n_pairs, HD, PAIR), f32),
-            pltpu.VMEM((n_pairs, HD, PAIR), f32),
+            pltpu.VMEM((heads, HD, HD), f32),
+            pltpu.VMEM((n_pairs, HD, HD), f32),
+            pltpu.VMEM((n_pairs, HD, HD), f32),
+            pltpu.VMEM((n_pairs, HD, HD), f32),
+            pltpu.VMEM((n_pairs, HD, HD), f32),
+            pltpu.VMEM((n_pairs, HD, HD), f32),
             pltpu.VMEM((n_cols, half, COLS), f32),
             dma((n_pairs,)), dma((4,)), dma((n_pairs,)), dma((n_cols,)),
             dma((n_pairs,)), dma((n_pairs,)), dma((n_pairs,)), dma((n_pairs,)),
+            dma((n_pairs,)), dma((n_pairs,)),
             dma((n_cols,)), dma((n_cols,)),
         ],
         compiler_params=pltpu.CompilerParams(

time: 59.3 us -> 45.3 us (0.76)
  Pallas kernels: 56.1 us -> 42 us
    pallas_call x1, Pallas kernels: 56.1 us -> 42 us  [body(): pl.pallas_call(functools.partial(kernel, n_seq), out_shape=jax.ShapeDtype...]
where the time goes in v2:
time: 45.3 us; the launch traced here: 45.1 us
  Pallas kernels  42 us (93%)
  local copies, waits for them, and re-layouts  3.13 us (7%)
    pallas_call x1, Pallas kernels, body(): pl.pallas_call(functools.partial(kernel, n_seq), out_shape=jax.ShapeDtype...  42 us
    unnamed x1, local copies, waits for them, and re-layouts  3.13 us

profile of v2, /device:TPU:27, one launch (start us, length us, event | category | flops | bytes accessed | tf_op | source)
XLA Modules:
  0.0 45.1 jit_solution(8939630662674667111)
XLA Ops:
  0.0 42.0 %shard_map.64 = bf16[256,4096]{1,0:T(8,128)(2,1)} custom-call(bf16[512,2048]{1,0:T(8,128)(2,1)} %q_hbm.1, bf16[512,256]{1,0:T(8,128)(2,1)} %k_hbm.1, bf16[512,256]{1,0:T(8,128)(2,1)} %v_hbm.1, bf16[16,128,128]{2,1,0:T(8,128)(2,1)} %fw_hbm.1, f32[16,128]{1,0:T(8,128)} %bitcast.1, bf16[2048,4096]{1,0:T(8,128)(2,1)} %w_hbm.1), custom_call_target="tpu_custom_call" | custom-call | flops 8589934592 | bytes 16777216 | tf_op jit(solution)/shard_map/pallas_call | solution.py:295
  42.0 3.1 %copy.8 = bf16[256,4096]{1,0:T(8,128)(2,1)} copy(bf16[256,4096]{1,0:T(8,128)(2,1)} %shard_map.64) | data formatting | bytes 4194304

commit v3 on v2

--- a/solution.py
+++ b/solution.py
@@ -19,11 +19,11 @@
 
 
 def kernel(
-    n_seq, q_hbm, k_hbm, v_hbm, fw_hbm, gain_hbm, w_hbm, out_hbm,
-    q_buf, k_buf, v_buf, fw_buf, gain_buf, w_buf, out_buf,
+    n_seq, q_hbm, k_hbm, v_hbm, fw_hbm, gain_hbm, w_hbm, out_ref,
+    q_buf, k_buf, v_buf, fw_buf, gain_buf, w_buf,
     vt_buf, fk_buf, fq_buf, intra_buf, nrm_buf, acc,
     s_buf, peer_s, p_buf, fwd, pre_out, pre_in, mp_recv,
-    q_sem, kv_sem, w_sem, out_sem,
+    q_sem, kv_sem, w_sem,
     y_send, y_recv, z_send, z_recv, b_send, b_recv, mp_send, mp_recv_sem,
 ):
     grp = lax.axis_index("groups")
@@ -90,10 +90,6 @@
             dst_ref=mp_recv.at[c], send_sem=mp_send.at[c],
             recv_sem=mp_recv_sem.at[c], device_id=peer, device_id_type=MESH)
 
-    def out_copy(c):
-        at = pl.multiple_of(c * COLS, COLS)
-        return pltpu.make_async_copy(out_buf.at[c], out_hbm.at[:, pl.ds(at, COLS)], out_sem.at[c])
-
     k_copy().start()
     fw_copy().start()
     v_copy().start()
@@ -264,8 +260,7 @@
         at = pl.multiple_of(c * COLS, COLS)
         total = acc[c, mine] + jnp.dot(nrm_buf[rest, mine], w_buf[rest, :, pl.ds(at, COLS)], preferred_element_type=jnp.float32)
         mp_copy(c).wait_recv()
-        out_buf[c] = (total + mp_recv[c]).astype(jnp.bfloat16)
-        out_copy(c).start()
+        out_ref[:, pl.ds(at, COLS)] = (total + mp_recv[c]).astype(jnp.bfloat16)
 
     @pl.loop(0, own_heads)
     def _(i):
@@ -279,7 +274,6 @@
     @pl.loop(0, n_cols)
     def _(c):
         mp_copy(c).wait_send()
-        out_copy(c).wait()
 
 
 def body(n_seq, queries, keys, values, feat_weight, head_gain, out_weight):
@@ -294,9 +288,9 @@
     dma = pltpu.SemaphoreType.DMA
     return pl.pallas_call(
         functools.partial(kernel, n_seq),
-        out_shape=jax.ShapeDtypeStruct((half, dout), bf),
+        out_shape=pltpu.VMEM((half, dout), bf),
         in_specs=[pl.BlockSpec(memory_space=pl.ANY)] * 6,
-        out_specs=pl.BlockSpec(memory_space=pl.ANY),
+        out_specs=pl.BlockSpec(memory_space=pltpu.VMEM),
         scratch_shapes=[
             pltpu.VMEM((n_pairs, rows, PAIR), bf),
             pltpu.VMEM(keys.shape, bf),
@@ -304,7 +298,6 @@
             pltpu.VMEM(feat_weight.shape, bf),
             pltpu.VMEM((heads, HD), f32),
             pltpu.VMEM((2, feats // 2, dout), bf),
-            pltpu.VMEM((n_cols, half, COLS), bf),
             pltpu.VMEM((keys.shape[1] // HD, HD, rows), bf),
             pltpu.VMEM((n_pairs, rows, PAIR), bf),
             pltpu.VMEM((n_pairs, rows, PAIR), bf),
@@ -318,13 +311,13 @@
             pltpu.VMEM((n_pairs, HD, HD), f32),
             pltpu.VMEM((n_pairs, HD, HD), f32),
             pltpu.VMEM((n_cols, half, COLS), f32),
-            dma((n_pairs,)), dma((4,)), dma((n_pairs,)), dma((n_cols,)),
+            dma((n_pairs,)), dma((4,)), dma((n_pairs,)),
             dma((n_pairs,)), dma((n_pairs,)), dma((n_pairs,)), dma((n_pairs,)),
             dma((n_pairs,)), dma((n_pairs,)),
             dma((n_cols,)), dma((n_cols,)),
         ],
         compiler_params=pltpu.CompilerParams(
-            collective_id=0, has_side_effects=True, vmem_limit_bytes=60 * 1024 * 1024),
+            collective_id=0, has_side_effects=True, vmem_limit_bytes=58 * 1024 * 1024),
         cost_estimate=pl.CostEstimate(
             flops=2 * rows * feats * dout, bytes_accessed=feats * dout * 2, transcendentals=0),
     )(queries, keys, values, feat_weight, gain, out_weight)

time: 45.3 us -> 42.8 us (0.945)
  local copies, waits for them, and re-layouts: 3.13 us -> 1.32 us
  Pallas kernels: 42 us -> 41.3 us
    unnamed x1, local copies, waits for them, and re-layouts: 3.13 us -> 1.32 us
    pallas_call x1, Pallas kernels: 42 us -> 41.3 us  [body(): pl.pallas_call(functools.partial(kernel, n_seq), out_shape=pltpu.VMEM((ha...]
where the time goes in v3:
time: 42.8 us; the launch traced here: 42.6 us
  Pallas kernels  41.3 us (96%)
  local copies, waits for them, and re-layouts  1.32 us (3%)
    pallas_call x1, Pallas kernels, body(): pl.pallas_call(functools.partial(kernel, n_seq), out_shape=pltpu.VMEM((ha...  41.3 us
    unnamed x1, local copies, waits for them, and re-layouts  1.32 us

profile of v3, /device:TPU:27, one launch (start us, length us, event | category | flops | bytes accessed | tf_op | source)
XLA Modules:
  0.0 42.6 jit_solution(16949661562389545639)
XLA Ops:
  0.0 41.3 %shard_map.64 = bf16[256,4096]{1,0:T(8,128)(2,1)S(1)} custom-call(bf16[512,2048]{1,0:T(8,128)(2,1)} %q_hbm.1, bf16[512,256]{1,0:T(8,128)(2,1)} %k_hbm.1, bf16[512,256]{1,0:T(8,128)(2,1)} %v_hbm.1, bf16[16,128,128]{2,1,0:T(8,128)(2,1)} %fw_hbm.1, f32[16,128]{1,0:T(8,128)} %bitcast.1, bf16[2048,4096]{1,0:T(8,128)(2,1)} %w_hbm.1), custom_call_target="tpu_custom_call" | custom-call | flops 8589934592 | bytes 16777216 | tf_op jit(solution)/shard_map/pallas_call | solution.py:289
  41.3 1.3 %copy.8 = bf16[256,4096]{1,0:T(8,128)(2,1)} copy(bf16[256,4096]{1,0:T(8,128)(2,1)S(1)} %shard_map.64) | data formatting | bytes 4194304
